TPU v7x, 32 devices: a whole 2x2x4 slice. The times are simulated.
32 devices in a mesh: dp: 16 (over z, y, x), mp: 2 (over core).
Axes of the slice: x: 2, y: 2, z: 4, core: 2. Of those that a mesh axis runs over, the one named last changes fastest.
Arguments:
- tokens: bfloat16 [32768, 768], P(('dp', 'mp')), may hold values from -6 to 6
- timesteps: int32 [256], P('dp'), may hold values from 0 to 1999
- src_len: int32 [256], P('dp'), may hold values from 1 to 64
- tgt_len: int32 [256], P('dp'), may hold values from 1 to 64
- sample_weight: float32 [256], P('dp'), may hold values from 0.25 to 4
- w_qkv: bfloat16 [3, 768, 768], P(None, None, 'mp'), may hold values from -0.21875 to 0.21875
- bias_qv: bfloat16 [2, 768], P(None, 'mp'), may hold values from -3 to 3
- w_out: bfloat16 [768, 768], P('mp'), may hold values from -1.25 to 1.25
- bias_out: float32 [768], replicated, may hold values from -2 to 2
- gain_attn: float32 [768], replicated, may hold values from 0.5 to 1.5
- shift_attn: float32 [768], replicated, may hold values from -3 to 3
- w_up: bfloat16 [768, 3072], P(None, 'mp'), may hold values from -0.21875 to 0.21875
- bias_up: bfloat16 [3072], P('mp'), may hold values from -3 to 3
- w_down: bfloat16 [3072, 768], P('mp'), may hold values from -0.109375 to 0.109375
- bias_down: float32 [768], replicated, may hold values from -2 to 2
- gain_mlp: float32 [768], replicated, may hold values from 0.5 to 1.5
- shift_mlp: float32 [768], replicated, may hold values from -3 to 3
- cotangent: bfloat16 [32768, 768], P(('dp', 'mp')), may hold values from -6 to 6
Outputs:
- layer_out: float32 [32768, 768], P(('dp', 'mp'))
- tokens_grad: float32 [32768, 768], P(('dp', 'mp'))
- grad_w_qkv: float32 [3, 768, 768], P(None, 'dp', 'mp')
- grad_w_out: float32 [768, 768], P(('mp', 'dp'))
- grad_w_up: float32 [768, 3072], P('dp', 'mp')
- grad_w_down: float32 [3072, 768], P(('mp', 'dp'))
- grad_bias_qv: float32 [2, 768], P(None, 'mp')
- grad_bias_up: float32 [3072], P('mp')
- grad_bias_out: float32 [768], replicated
- grad_rows: float32 [5, 768], replicated
Inputs may be any that keep to these rules, and one draw needn't show every extreme that they name: A sequence holds src_len source tokens, then tgt_len target tokens, then padding.
All inputs are finite; a program needn't handle non-finite values.
Results may differ from a plain program's by a relative error of at most 0.018.
The roundings to bfloat16 on the way count: a program that leaves them out, or rounds other values in their place, can miss the bound.
Values may be sent and summed in bfloat16 or wider, within the bound.
No kernel may reach another device: no remote copies, remote signals or barrier semaphores. Data moves between devices by JAX's collectives and lax.ppermute only.
A program may use at most 192 MiB of HBM per device.

v0:
```python
import math

import jax
import jax.numpy as jnp
from jax import lax
from jax.sharding import PartitionSpec as P

HD = 64
LEN = 128


NORM_EPS = 1e-05
MASK_FILL = -1e30


def time_table(timesteps, width):
    half_width = width // 2
    frequency = jnp.exp(-math.log(10000.0) * jnp.arange(half_width, dtype=jnp.float32) / half_width)
    angles = timesteps.astype(jnp.float32)[:, None] * frequency[None, :]
    return jnp.concatenate([jnp.sin(angles), jnp.cos(angles)], axis=1)


def norm_forward(value, gain_vec, shift_vec):
    row_mean = jnp.mean(value, axis=1, keepdims=True)
    centred = value - row_mean
    inv_std = lax.rsqrt(jnp.mean(centred * centred, axis=1, keepdims=True) + NORM_EPS)
    normed = centred * inv_std
    return (normed * gain_vec + shift_vec, normed, inv_std)


def norm_backward(grad_in, normed, inv_std, gain_vec):
    scaled = grad_in * gain_vec
    inner = (
        scaled
        - jnp.mean(scaled, axis=1, keepdims=True)
        - normed * jnp.mean(scaled * normed, axis=1, keepdims=True)
    )
    return (inv_std * inner, jnp.sum(grad_in * normed, axis=0), jnp.sum(grad_in, axis=0))


def gelu_exact(value):
    return jax.nn.gelu(value, approximate=False)


def split_heads(matrix):
    row_count, col_count = matrix.shape
    return matrix.reshape(row_count // LEN, LEN, col_count // HD, HD)


def score_block(queries, keys_low, lengths):
    scores = jnp.einsum(
        "gqhe,gkhe->ghqk",
        split_heads(queries),
        split_heads(keys_low),
        preferred_element_type=jnp.float32,
    ) * HD ** (-0.5)
    live_keys = (jnp.arange(LEN)[None, :] < lengths[:, None])[:, None, None, :]
    return jnp.where(live_keys, scores, MASK_FILL)


def attend(queries, keys_low, values, lengths):
    scores = score_block(queries, keys_low, lengths)
    row_max = jnp.max(scores, axis=3, keepdims=True)
    total = jnp.sum(jnp.exp(scores - row_max), axis=3, keepdims=True)
    log_total = row_max + jnp.log(total)
    probs_low = jnp.exp(scores - log_total).astype(jnp.bfloat16)
    context = jnp.einsum(
        "ghqk,gkhe->gqhe", probs_low, split_heads(values), preferred_element_type=jnp.float32
    )
    return (context.reshape(queries.shape).astype(jnp.bfloat16), log_total)


def attend_backward(queries, keys_low, values, lengths, log_total, grad_context):
    probs = jnp.exp(score_block(queries, keys_low, lengths) - log_total)
    grad_heads = split_heads(grad_context)
    grad_values = jnp.einsum(
        "ghqk,gqhe->gkhe",
        probs.astype(jnp.bfloat16),
        grad_heads,
        preferred_element_type=jnp.float32,
    )
    grad_probs = jnp.einsum(
        "gqhe,gkhe->ghqk", grad_heads, split_heads(values), preferred_element_type=jnp.float32
    )
    grad_scores = (
        probs * (grad_probs - jnp.sum(probs * grad_probs, axis=3, keepdims=True))
    ).astype(jnp.bfloat16)
    grad_queries = jnp.einsum(
        "ghqk,gkhe->gqhe", grad_scores, split_heads(keys_low), preferred_element_type=jnp.float32
    ) * HD ** (-0.5)
    grad_keys = jnp.einsum(
        "ghqk,gqhe->gkhe", grad_scores, split_heads(queries), preferred_element_type=jnp.float32
    ) * HD ** (-0.5)
    flat_shape = queries.shape
    return jnp.stack(
        [
            grad_queries.reshape(flat_shape),
            grad_keys.reshape(flat_shape),
            grad_values.reshape(flat_shape),
        ]
    ).astype(jnp.bfloat16)


def per_device(
    tokens,
    timesteps,
    src_len,
    tgt_len,
    sample_weight,
    w_qkv,
    bias_qv,
    w_out,
    bias_out,
    gain_attn,
    shift_attn,
    w_up,
    bias_up,
    w_down,
    bias_down,
    gain_mlp,
    shift_mlp,
    cotangent,
):
    row_count, width = tokens.shape
    mp_count = lax.axis_size("mp")
    mp_index = lax.axis_index("mp")
    seq_local = row_count // LEN
    own_start = mp_index * seq_local
    lengths_all = src_len + tgt_len
    own_steps = lax.dynamic_slice_in_dim(timesteps, own_start, seq_local)
    own_src = lax.dynamic_slice_in_dim(src_len, own_start, seq_local)
    own_len = lax.dynamic_slice_in_dim(lengths_all, own_start, seq_local)
    own_weight = lax.dynamic_slice_in_dim(sample_weight, own_start, seq_local)
    start_x = (
        tokens.astype(jnp.float32).reshape(seq_local, LEN, width)
        + time_table(own_steps, width)[:, None, :]
    ).reshape(row_count, width)
    position = jnp.arange(LEN)[None, :]
    target_scale = ((position >= own_src[:, None]) & (position < own_len[:, None])).astype(
        jnp.float32
    ) * own_weight[:, None]
    out_grad = (
        cotangent.astype(jnp.float32).reshape(seq_local, LEN, width) * target_scale[:, :, None]
    ).reshape(row_count, width)
    x_low = start_x.astype(jnp.bfloat16)
    col_local = bias_qv.shape[1]
    ff_local = bias_up.shape[0]
    x_all = lax.all_gather(x_low, "mp", axis=0, tiled=True)
    qkv_w, out_w, up_w, down_w, qv_bias, up_bias = (w_qkv, w_out, w_up, w_down, bias_qv, bias_up)
    projected = jnp.einsum("td,sde->ste", x_all, qkv_w, preferred_element_type=jnp.float32)
    queries = (projected[0] + qv_bias[0]).astype(jnp.bfloat16)
    keys_low = projected[1].astype(jnp.bfloat16)
    values = (projected[2] + qv_bias[1]).astype(jnp.bfloat16)
    context, log_total = attend(queries, keys_low, values, lengths_all)
    attn_out = lax.psum_scatter(
        jnp.dot(context, out_w, preferred_element_type=jnp.float32),
        "mp",
        scatter_dimension=0,
        tiled=True,
    )
    mid_x, normed_attn, inv_attn = norm_forward(
        start_x + attn_out + bias_out, gain_attn, shift_attn
    )
    mid_low = mid_x.astype(jnp.bfloat16)
    mid_all = lax.all_gather(mid_low, "mp", axis=0, tiled=True)
    pre_act = jnp.dot(mid_all, up_w, preferred_element_type=jnp.float32) + up_bias
    hidden = gelu_exact(pre_act).astype(jnp.bfloat16)
    mlp_out = lax.psum_scatter(
        jnp.dot(hidden, down_w, preferred_element_type=jnp.float32),
        "mp",
        scatter_dimension=0,
        tiled=True,
    )
    layer_out, normed_mlp, inv_mlp = norm_forward(mid_x + mlp_out + bias_down, gain_mlp, shift_mlp)
    out_in_grad, grad_gain_mlp, grad_shift_mlp = norm_backward(
        out_grad, normed_mlp, inv_mlp, gain_mlp
    )
    mlp_grad_low = out_in_grad.astype(jnp.bfloat16)
    mlp_grad_all = lax.all_gather(mlp_grad_low, "mp", axis=0, tiled=True)
    grad_hidden = jnp.dot(mlp_grad_all, down_w.T, preferred_element_type=jnp.float32)
    gelu_pull = jax.vjp(gelu_exact, pre_act)[1]
    pre_grad = gelu_pull(grad_hidden)[0].astype(jnp.bfloat16)
    mid_part = lax.psum_scatter(
        jnp.dot(pre_grad, up_w.T, preferred_element_type=jnp.float32),
        "mp",
        scatter_dimension=0,
        tiled=True,
    )
    mid_in_grad, grad_gain_attn, grad_shift_attn = norm_backward(
        mid_part + out_in_grad, normed_attn, inv_attn, gain_attn
    )
    attn_grad_low = mid_in_grad.astype(jnp.bfloat16)
    attn_grad_all = lax.all_gather(attn_grad_low, "mp", axis=0, tiled=True)
    grad_context = jnp.dot(attn_grad_all, out_w.T, preferred_element_type=jnp.float32).astype(
        jnp.bfloat16
    )
    grad_qkv_low = attend_backward(queries, keys_low, values, lengths_all, log_total, grad_context)
    input_part = lax.psum_scatter(
        jnp.einsum("ste,sde->td", grad_qkv_low, qkv_w, preferred_element_type=jnp.float32).astype(
            jnp.bfloat16
        ),
        "mp",
        scatter_dimension=0,
        tiled=True,
    ).astype(jnp.float32)
    tokens_grad = input_part + mid_in_grad
    grad_w_qkv, grad_w_out, grad_w_up, grad_w_down = (
        lax.psum_scatter(
            jnp.einsum("td,ste->sde", x_all, grad_qkv_low, preferred_element_type=jnp.float32),
            "dp",
            scatter_dimension=1,
            tiled=True,
        ),
        lax.psum_scatter(
            jnp.dot(context.T, attn_grad_all, preferred_element_type=jnp.float32),
            "dp",
            scatter_dimension=0,
            tiled=True,
        ),
        lax.psum_scatter(
            jnp.dot(mid_all.T, pre_grad, preferred_element_type=jnp.float32),
            "dp",
            scatter_dimension=0,
            tiled=True,
        ),
        lax.psum_scatter(
            jnp.dot(hidden.T, mlp_grad_all, preferred_element_type=jnp.float32),
            "dp",
            scatter_dimension=0,
            tiled=True,
        ),
    )
    qv_full = lax.dynamic_update_slice(
        jnp.zeros((2, width), jnp.float32),
        jnp.stack(
            [
                jnp.sum(grad_qkv_low[0].astype(jnp.float32), axis=0),
                jnp.sum(grad_qkv_low[2].astype(jnp.float32), axis=0),
            ]
        ),
        (0, mp_index * col_local),
    )
    up_full = lax.dynamic_update_slice(
        jnp.zeros((ff_local * mp_count,), jnp.float32),
        jnp.sum(pre_grad.astype(jnp.float32), axis=0),
        (mp_index * ff_local,),
    )
    out_bias_term = jnp.sum(attn_grad_low.astype(jnp.float32), axis=0)
    row_terms = jnp.stack(
        [
            grad_gain_attn,
            grad_shift_attn,
            jnp.sum(mlp_grad_low.astype(jnp.float32), axis=0),
            grad_gain_mlp,
            grad_shift_mlp,
        ]
    )
    grad_rows, grad_bias_out, qv_summed, up_summed = lax.psum(
        (row_terms, out_bias_term, qv_full, up_full), ("dp", "mp")
    )
    grad_bias_qv = lax.dynamic_slice_in_dim(qv_summed, mp_index * col_local, col_local, 1)
    grad_bias_up = lax.dynamic_slice_in_dim(up_summed, mp_index * ff_local, ff_local, 0)
    return (
        layer_out,
        tokens_grad,
        grad_w_qkv,
        grad_w_out,
        grad_w_up,
        grad_w_down,
        grad_bias_qv,
        grad_bias_up,
        grad_bias_out,
        grad_rows,
    )


def solution(mesh):
    in_specs = (
        P(("dp", "mp"), None),
        P("dp"),
        P("dp"),
        P("dp"),
        P("dp"),
        P(None, None, "mp"),
        P(None, "mp"),
        P("mp", None),
        P(),
        P(),
        P(),
        P(None, "mp"),
        P("mp"),
        P("mp", None),
        P(),
        P(),
        P(),
        P(("dp", "mp"), None),
    )
    out_specs = (
        P(("dp", "mp"), None),
        P(("dp", "mp"), None),
        P(None, "dp", "mp"),
        P(("mp", "dp"), None),
        P("dp", "mp"),
        P(("mp", "dp"), None),
        P(None, "mp"),
        P("mp"),
        P(),
        P(),
    )
    return jax.shard_map(
        per_device, mesh=mesh, in_specs=in_specs, out_specs=out_specs, check_vma=False
    )
```

profile of v0, /device:TPU:0, one launch (start us, length us, event | category | flops | bytes accessed | tf_op | source)
XLA Modules:
  0.0 944.2 jit_solution(4707678321671163142)
XLA Ops:
  8.3 2.8 fusion.14
  11.5 14.7 %all-gather.5.cloned.1.call-done = bf16[2048,768]{1,0:T(8,128)(2,1)} async-done(((bf16[1024,768]{1,0:T(8,128)(2,1)}), bf16[2048,768]{1,0:T(8,128)(2,1)}) %all-gather.5.cloned.1.call-update) | async-done | bytes 3145744 | tf_op jit(solution)/shard_map/all_gather | solution.py:148
  26.2 6.8 convolution_bitcast_fusion
  33.0 3.1 fusion.55
  37.4 3.7 copy.66
  41.1 4.2 copy.97
  45.3 2.6 copy.67
  47.9 2.0 copy.98
  50.7 3.0 fusion.6
  53.7 1.8 exponential_reduce_fusion
  56.4 3.6 copy.65
  60.0 2.7 copy.96
  63.7 2.5 fusion.23
  68.5 4.5 fusion.21
  73.0 15.8 %reduce-scatter.8.cloned.1.call-done = f32[1024,768]{1,0:T(8,128)} async-done(((f32[2048,768]{1,0:T(8,128)}), f32[1024,768]{1,0:T(8,128)}) %reduce-scatter.8.cloned.1.call-update) | async-done | bytes 3145744 | tf_op jit(solution)/shard_map/reduce_scatter | solution.py:155
  88.8 2.9 fusion.54
  95.2 13.4 %all-gather.7.cloned.1.call-done = bf16[2048,768]{1,0:T(8,128)(2,1)} async-done(((bf16[1024,768]{1,0:T(8,128)(2,1)}), bf16[2048,768]{1,0:T(8,128)(2,1)}) %all-gather.7.cloned.1.call-update) | async-done | bytes 3145744 | tf_op jit(solution)/shard_map/all_gather | solution.py:165
  108.6 34.0 %multiply_convert_fusion = (bf16[2048,1536]{1,0:T(8,128)(2,1)S(1)}, f32[2048,1536]{1,0:T(8,128)}, f32[2048,1536]{1,0:T(8,128)}) fusion(f32[1536]{0:T(1024)S(1)} %convert_element_type.102, bf16[2048,768]{1,0:T(8,128)(2,1)} %all-gather.7.cloned.1.call-done, bf16[768,1536]{1,0:T(8,128)(2,1)S(1)} %copy-done), kind=kOutput, calls=%fused_computation.4 | convolution fusion | flops 5039456256 | bytes 36968448 | tf_op jit(solution)/shard_map/dot_general | solution.py:166
  142.6 2.7 copy-done.37
  145.3 6.9 fusion.56
  153.2 14.9 %reduce-scatter.10.cloned.1.call-done = f32[1024,768]{1,0:T(8,128)} async-done(((f32[2048,768]{1,0:T(8,128)}), f32[1024,768]{1,0:T(8,128)}) %reduce-scatter.10.cloned.1.call-update) | async-done | bytes 3145744 | tf_op jit(solution)/shard_map/reduce_scatter | solution.py:168
  168.1 3.9 fusion.52
  172.5 2.0 copy-done.6
  174.5 1.8 multiply_reduce_fusion.1
  176.4 2.2 convert_reduce_fusion.1
  178.7 13.4 %all-gather.9.cloned.1.call-done = bf16[2048,768]{1,0:T(8,128)(2,1)} async-done(((bf16[1024,768]{1,0:T(8,128)(2,1)}), bf16[2048,768]{1,0:T(8,128)(2,1)}) %all-gather.9.cloned.1.call-update) | async-done | bytes 3145744 | tf_op jit(solution)/shard_map/all_gather | solution.py:179
  192.1 17.3 %convert_reduce_fusion = (f32[1536]{0:T(1024)S(1)}, bf16[2048,1536]{1,0:T(8,128)(2,1)S(1)}) fusion(f32[2048,1536]{1,0:T(8,128)} %get-tuple-element.63, bf16[2048,768]{1,0:T(8,128)(2,1)} %all-gather.9.cloned.1.call-done, bf16[1536,768]{1,0:T(8,128)(2,1)} %param.31, f32[2048,1536]{1,0:T(8,128)} %get-tuple-element.73, f32[1536]{0:T(1024)S(1)} %convert_element_type.102), kind=kOutput, calls=%fused_computation.2 | convolution fusion | flops 4885314048 | bytes 36974592 | tf_op jit(solution)/shard_map/dot_general | solution.py:180
  209.4 2.6 copy-done.38
  212.0 6.9 fusion.57
  219.0 15.8 %reduce-scatter.12.cloned.1.call-done = f32[1024,768]{1,0:T(8,128)} async-done(((f32[2048,768]{1,0:T(8,128)}), f32[1024,768]{1,0:T(8,128)}) %reduce-scatter.12.cloned.1.call-update) | async-done | bytes 3145744 | tf_op jit(solution)/shard_map/reduce_scatter | solution.py:183
  234.8 6.9 multiply_reduce_fusion.2
  241.7 2.8 convert_reduce_fusion.2
  244.6 13.4 %all-gather.11.cloned.1.call-done = bf16[2048,768]{1,0:T(8,128)(2,1)} async-done(((bf16[1024,768]{1,0:T(8,128)(2,1)}), bf16[2048,768]{1,0:T(8,128)(2,1)}) %all-gather.11.cloned.1.call-update) | async-done | bytes 3145744 | tf_op jit(solution)/shard_map/all_gather | solution.py:193
  258.0 4.9 convolution_convert_fusion
  262.8 2.8 copy.73
  265.6 2.0 copy.100
  267.6 6.1 multiply_reduce_fusion
  273.8 3.6 fusion.24
  277.4 2.3 multiply_convert_fusion.1
  281.1 3.4 fusion.26
  284.5 2.2 copy.78
  286.7 3.7 stack_reshape.12
  290.3 3.6 copy.84
  293.9 3.7 stack_reshape.14
  297.6 2.6 copy.85
  300.2 3.6 copy.81
  303.7 3.7 stack_reshape.13
  307.4 2.6 copy.86
  310.0 2.8 copy.87
  312.8 9.1 fusion.16
  321.9 6.3 copy.89
  328.3 9.0 bitcast_convert_fusion
  337.4 9.6 %fusion.59 = f32[1536,768]{1,0:T(8,128)} fusion(bf16[2048,1536]{1,0:T(8,128)(2,1)} %copy-done.37, bf16[2048,768]{1,0:T(8,128)(2,1)} %all-gather.9.cloned.1.call-done), kind=kOutput, calls=%fused_computation.125 | convolution fusion | flops 4831838208 | bytes 14155776 | tf_op jit(solution)/shard_map/dot_general | solution.py:227
  347.1 10.0 %fusion.58 = f32[768,1536]{1,0:T(8,128)} fusion(bf16[2048,768]{1,0:T(8,128)(2,1)} %all-gather.7.cloned.1.call-done, bf16[2048,1536]{1,0:T(8,128)(2,1)} %copy-done.38), kind=kOutput, calls=%fused_computation.124 | convolution fusion | flops 4831838208 | bytes 14155776 | tf_op jit(solution)/shard_map/dot_general | solution.py:221
  357.1 4.9 fusion.19
  363.8 1.7 convert_reduce_fusion.4
  365.5 1.7 convert_reduce_fusion.3
  367.2 42.4 %all-reduce.1 = (f32[2,768]{1,0:T(2,128)S(1)}, f32[3072]{0:T(1024)S(1)}, f32[768]{0:T(1024)}, f32[5,768]{1,0:T(8,128)}) all-reduce(f32[2,768]{1,0:T(2,128)S(1)} %maximum_dynamic-update-slice_fusion, f32[3072]{0:T(1024)S(1)} %dynamic_update_slice.7, f32[768]{0:T(1024)S(1)} %get-tuple-element.56, ...), channel_id=1, replica_groups=mesh['dp'=16,'mp'=2] {'dp','mp'}, use_global_device_ids=true, to_apply=%region_21.22 | all-reduce | flops 9216 | bytes 73728 | tf_op jit(solution)/shard_map/psum | solution.py:258
  410.8 98.7 %all-reduce.4.cloned.1.call-done = f32[3,768,384]{2,0,1:T(4,128)} async-done(((f32[3,768,384]{2,0,1:T(4,128)}), f32[3,768,384]{2,0,1:T(4,128)}) %all-reduce.4.cloned.1.call-update) | async-done | bytes 3538960
  511.2 10.5 %reduce-scatter.14.cloned.1.call-done = bf16[1024,768]{1,0:T(8,128)(2,1)} async-done(((bf16[2048,768]{1,0:T(8,128)(2,1)}), bf16[1024,768]{1,0:T(8,128)(2,1)}) %reduce-scatter.14.cloned.1.call-update) | async-done | bytes 1572880 | tf_op jit(solution)/shard_map/reduce_scatter | solution.py:198
  521.7 4.3 convert_add_fusion
  526.0 140.5 %reduce-scatter.20.cloned.1.call-done = f32[96,768]{1,0:T(8,128)} async-done(((f32[1536,768]{1,0:T(8,128)}), f32[96,768]{1,0:T(8,128)}) %reduce-scatter.20.cloned.1.call-update) | async-done | bytes 294928 | tf_op jit(solution)/shard_map/reduce_scatter | solution.py:226
  666.6 142.1 %reduce-scatter.18.cloned.1.call-done = f32[48,1536]{1,0:T(8,128)} async-done(((f32[768,1536]{1,0:T(8,128)}), f32[48,1536]{1,0:T(8,128)}) %reduce-scatter.18.cloned.1.call-update) | async-done | bytes 294928 | tf_op jit(solution)/shard_map/reduce_scatter | solution.py:220
  808.7 128.4 %reduce-scatter.16.cloned.1.call-done = f32[24,768]{1,0:T(8,128)} async-done(((f32[384,768]{1,0:T(8,128)}), f32[24,768]{1,0:T(8,128)}) %reduce-scatter.16.cloned.1.call-update) | async-done | bytes 73744 | tf_op jit(solution)/shard_map/reduce_scatter | solution.py:214
  (151 shorter events, 18.5 us)
Async XLA Ops:
  7.2 101.4 %copy-start = (bf16[768,1536]{1,0:T(8,128)(2,1)S(1)}, bf16[768,1536]{1,0:T(8,128)(2,1)}, u32[]{:S(2)}) copy-start(bf16[768,1536]{1,0:T(8,128)(2,1)} %param.29) | copy-start | bytes 7077892
  7.2 4.0 copy-start.24
  7.2 4.2 copy-start.33
  7.2 4.2 copy-start.32
  7.2 18.9 %all-gather.5.cloned.1.call-start = ((), (), s32[]{:S(2)}) async-start(), calls=%async_computation.7 | async-start | bytes 4718592 | tf_op jit(solution)/shard_map/all_gather | solution.py:148
  11.2 77.6 %reduce-scatter.8.cloned.1.call-start = ((), (), s32[]{:S(2)}) async-start(), calls=%async_computation.8 | async-start | bytes 9437184 | tf_op jit(solution)/shard_map/reduce_scatter | solution.py:155
  11.4 21.5 %copy-start.29 = (s32[16]{0:T(128)}, s32[16]{0:T(128)S(1)}, u32[]{:S(2)}) copy-start(s32[16]{0:T(128)S(1)} %add.162) | copy-start | bytes 196
  11.5 51.7 %copy-start.21 = (pred[16,128]{1,0:T(8,128)(4,1)}, pred[16,128]{1,0:T(8,128)(4,1)S(1)}, u32[]{:S(2)}) copy-start(pred[16,128]{1,0:T(8,128)(4,1)S(1)} %iota_compare_fusion) | copy-start | bytes 6148
  47.9 2.4 copy-start.7
  49.8 3.8 copy-start.11
  50.7 3.0 copy-start.13
  53.7 2.7 copy-start.4
  56.4 6.8 copy-start.15
  60.0 3.7 copy-start.5
  63.7 2.5 copy-start.9
  66.2 2.2 copy-start.17
  67.3 1.2 copy-start.8
  73.0 15.8 %copy-start.25 = (f32[768]{0:T(1024)S(1)}, f32[768]{0:T(1024)}, u32[]{:S(2)}) copy-start(f32[768]{0:T(1024)} %param.26) | copy-start | bytes 9220
  73.0 35.6 %all-gather.7.cloned.1.call-start = ((), (), s32[]{:S(2)}) async-start(), calls=%async_computation.9 | async-start | bytes 4718592 | tf_op jit(solution)/shard_map/all_gather | solution.py:165
  91.7 1.7 copy-start.1
  91.8 1.7 copy-start.19
  91.8 1.6 copy-start.23
  93.4 1.8 copy-start.28
  95.1 72.9 %reduce-scatter.10.cloned.1.call-start = ((), (), s32[]{:S(2)}) async-start(), calls=%async_computation.10 | async-start | bytes 9437184 | tf_op jit(solution)/shard_map/reduce_scatter | solution.py:168
  108.6 36.7 %copy-start.31 = (bf16[1536,768]{1,0:T(8,128)(2,1)S(1)}, bf16[1536,768]{1,0:T(8,128)(2,1)}, u32[]{:S(2)}) copy-start(bf16[1536,768]{1,0:T(8,128)(2,1)} %param.31) | copy-start | bytes 7077892
  142.6 2.7 copy-start.37
  152.2 0.7 copy-start.30
  152.2 0.7 copy-start.34
  152.2 0.8 copy-start.35
  152.2 15.9 %copy-start.26 = (f32[768]{0:T(1024)S(1)}, f32[768]{0:T(1024)}, u32[]{:S(2)}) copy-start(f32[768]{0:T(1024)} %param.32) | copy-start | bytes 9220
  152.2 39.9 %all-gather.9.cloned.1.call-start = ((), (), s32[]{:S(2)}) async-start(), calls=%async_computation.11 | async-start | bytes 4718592 | tf_op jit(solution)/shard_map/all_gather | solution.py:179
  171.9 4.4 copy-start.3
  172.0 2.5 copy-start.6
  172.0 2.5 copy-start.20
  178.7 56.2 %reduce-scatter.12.cloned.1.call-start = ((), (), s32[]{:S(2)}) async-start(), calls=%async_computation.12 | async-start | bytes 9437184 | tf_op jit(solution)/shard_map/reduce_scatter | solution.py:183
  209.4 2.7 copy-start.38
  218.9 15.9 %copy-start.27 = (f32[768]{0:T(1024)S(1)}, f32[768]{0:T(1024)}, u32[]{:S(2)}) copy-start(f32[768]{0:T(1024)} %param.34) | copy-start | bytes 9220
  219.0 39.0 %all-gather.11.cloned.1.call-start = ((), (), s32[]{:S(2)}) async-start(), calls=%async_computation.13 | async-start | bytes 4718592 | tf_op jit(solution)/shard_map/all_gather | solution.py:193
  234.8 6.9 copy-start.2
  241.7 16.3 %copy-start.18 = (bf16[384,768]{1,0:T(8,128)(2,1)S(1)}, bf16[384,768]{1,0:T(8,128)(2,1)}, u32[]{:S(2)}) copy-start(bf16[384,768]{1,0:T(8,128)(2,1)} %param.25) | copy-start | bytes 1769476
  244.5 265.0 %all-reduce.4.cloned.1.call-start = ((), (), s32[]{:S(2)}) async-start(), calls=%async_computation.18 | async-start | bytes 9437184
  262.8 4.8 copy-start.16
  262.8 4.8 copy-start.22
  265.6 2.0 copy-start.10
  265.6 8.1 slice-start
  267.6 6.1 slice-start.1
  277.4 2.3 copy-start.12
  279.7 1.4 copy-start.14
  328.3 193.4 %reduce-scatter.14.cloned.1.call-start = ((), (), s32[]{:S(2)}) async-start(), calls=%async_computation.14 | async-start | bytes 4718592 | tf_op jit(solution)/shard_map/reduce_scatter | solution.py:198
  337.4 329.2 %reduce-scatter.20.cloned.1.call-start = ((), (), s32[]{:S(2)}) async-start(), calls=%async_computation.17 | async-start | bytes 5013504 | tf_op jit(solution)/shard_map/reduce_scatter | solution.py:226
  347.0 461.7 %reduce-scatter.18.cloned.1.call-start = ((), (), s32[]{:S(2)}) async-start(), calls=%async_computation.16 | async-start | bytes 5013504 | tf_op jit(solution)/shard_map/reduce_scatter | solution.py:220
  357.1 5.0 copy-start.36
  357.1 580.0 %reduce-scatter.16.cloned.1.call-start = ((), (), s32[]{:S(2)}) async-start(), calls=%async_computation.15 | async-start | bytes 1253376 | tf_op jit(solution)/shard_map/reduce_scatter | solution.py:214
Sparse Core Ops, SparseCore 0:
  11.3 14.8 all-gather.4
  73.1 15.6 reduce-scatter.7
  95.3 13.2 all-gather.6
  152.4 15.6 reduce-scatter.9
  178.8 13.2 all-gather.8
  219.1 15.6 reduce-scatter.11
  244.7 13.2 all-gather.10
  328.4 181.0 all-reduce.3
  511.7 9.9 reduce-scatter.13
  528.1 138.3 reduce-scatter.19
  672.3 136.3 reduce-scatter.17
  814.6 122.4 reduce-scatter.15
where the time goes:
time: 949 us; the launch traced here: 944 us
  waiting for transfers between devices  622 us (66%)
  matrix products  143 us (15%)
  local copies, waits for them, and re-layouts  80.4 us (8%)
  blocking collectives  42.4 us (4%)
  other arithmetic  40.1 us (4%)
  between operations  15.8 us (2%)
    reduce_scatter x1, waiting for transfers between devices, per_device(): lax.psum_scatter(jnp.dot(mid_all.T, pre_grad, preferred_element_type=jnp....  142 us
    reduce_scatter x1, waiting for transfers between devices, per_device(): lax.psum_scatter(jnp.dot(hidden.T, mlp_grad_all, preferred_element_type=j...  141 us
    reduce_scatter x1, waiting for transfers between devices, per_device(): lax.psum_scatter(jnp.dot(context.T, attn_grad_all, preferred_element_type...  128 us
    unnamed x13, waiting for transfers between devices  98.9 us
    psum x1, blocking collectives, per_device(): lax.psum((row_terms, out_bias_term, qv_full, up_full), ('dp', 'mp'))  42.4 us
    dot_general x1, matrix products, per_device(): jnp.dot(mid_all, up_w, preferred_element_type=jnp.float32) + up_bias  34 us
    unnamed x89, local copies, waits for them, and re-layouts  25.7 us
    another operation x6, local copies, waits for them, and re-layouts, attend_backward(): jnp.stack([grad_queries.reshape(flat_shape), grad_keys.reshape(flat_shape...  19 us
  transfers between devices with their start and end apart: 12, of which 12 were waited for; matrix products, arithmetic and copies ran while one was open for 5% of the time, Pallas kernels for 0%

commit v1 on v0

v1 whole, which is shorter than its diff:
```python
import functools
import math

import jax
import jax.numpy as jnp
from jax import lax
from jax.experimental import pallas as pl
from jax.experimental.pallas import tpu as pltpu
from jax.sharding import PartitionSpec as P

HD = 64
LEN = 128
PAIR = 2 * HD
NORM_EPS = 1e-05
MASK_FILL = -1e30
BF = jnp.bfloat16
F32 = jnp.float32
MIB = 1 << 20

NN = (((1,), (0,)), ((), ()))
NT = (((1,), (1,)), ((), ()))
TN = (((0,), (0,)), ((), ()))

VMEM_SPEC = pl.BlockSpec(memory_space=pltpu.VMEM)
SMEM_SPEC = pl.BlockSpec(memory_space=pltpu.SMEM)


def mm(a, b, dims=NN):
    return lax.dot_general(a, b, dims, preferred_element_type=F32)


def fixed(shape):
    zeros = (0,) * len(shape)
    return pl.BlockSpec(shape, lambda *_: zeros)


def params(mib):
    return pltpu.CompilerParams(vmem_limit_bytes=mib * MIB)


def time_table(timesteps, width):
    half_width = width // 2
    frequency = jnp.exp(-math.log(10000.0) * jnp.arange(half_width, dtype=F32) / half_width)
    angles = timesteps.astype(F32)[:, None] * frequency[None, :]
    return jnp.concatenate([jnp.sin(angles), jnp.cos(angles)], axis=1)


def add_table(tok_ref, table_ref, first_seq, count):
    rows = []
    for s in range(count):
        part = tok_ref[s * LEN : (s + 1) * LEN, :].astype(F32)
        rows.append(part + table_ref[pl.ds(first_seq + s, 1), :])
    return jnp.concatenate(rows, axis=0)


def half_masks(rows, value=1.0):
    lane = lax.broadcasted_iota(jnp.int32, (rows, PAIR), 1)
    first = jnp.where(lane < HD, value, 0.0).astype(BF)
    second = jnp.where(lane < HD, 0.0, value).astype(BF)
    return first, second


def fold8(value):
    rows, cols = value.shape
    return jnp.sum(value.reshape(rows // 8, 8, cols), axis=0)


def attend_kernel(seqs, emit_x, len_ref, tok_ref, table_ref, w_ref, bias_ref, *outs):
    if emit_x:
        qkv_ref, prob_ref, ctx_ref, x_ref = outs
    else:
        qkv_ref, prob_ref, ctx_ref = outs
    first_seq = pl.program_id(0) * seqs
    x_low = add_table(tok_ref, table_ref, first_seq, seqs).astype(BF)
    if emit_x:
        x_ref[...] = x_low
    q = (mm(x_low, w_ref[0]) + bias_ref[0:1, :]).astype(BF)
    k = mm(x_low, w_ref[1]).astype(BF)
    v = (mm(x_low, w_ref[2]) + bias_ref[1:2, :]).astype(BF)
    qkv_ref[0] = q
    qkv_ref[1] = k
    qkv_ref[2] = v
    scale_a, scale_b = half_masks(LEN, HD**-0.5)
    one_a, one_b = half_masks(LEN)
    key_pos = lax.broadcasted_iota(jnp.int32, (LEN, 2 * LEN), 1) % LEN
    for s in range(seqs):
        live = key_pos < len_ref[first_seq + s]
        rows = slice(s * LEN, (s + 1) * LEN)
        for j in range(q.shape[1] // PAIR):
            cols = slice(j * PAIR, (j + 1) * PAIR)
            q2, k2, v2 = q[rows, cols], k[rows, cols], v[rows, cols]
            kcat = jnp.concatenate([k2 * scale_a, k2 * scale_b], axis=0)
            vcat = jnp.concatenate([v2 * one_a, v2 * one_b], axis=0)
            scores = jnp.where(live, mm(q2, kcat, NT), MASK_FILL)
            halves = []
            for h in range(2):
                part = scores[:, h * LEN : (h + 1) * LEN]
                e = jnp.exp(part - jnp.max(part, axis=1, keepdims=True))
                halves.append(e / jnp.sum(e, axis=1, keepdims=True))
            probs = jnp.concatenate(halves, axis=1)
            prob_ref[s, j] = probs
            ctx_ref[rows, cols] = mm(probs.astype(BF), vcat).astype(BF)


def attend(tokens, table, lengths, w_half, bias_half, emit_x):
    rows, width = tokens.shape
    cols = w_half.shape[2]
    seqs = 2
    block = seqs * LEN
    pairs = cols // PAIR
    out_shape = [
        jax.ShapeDtypeStruct((3, rows, cols), BF),
        jax.ShapeDtypeStruct((rows // LEN, pairs, LEN, 2 * LEN), F32),
        jax.ShapeDtypeStruct((rows, cols), BF),
    ]
    out_specs = [
        pl.BlockSpec((3, block, cols), lambda i: (0, i, 0)),
        pl.BlockSpec((seqs, pairs, LEN, 2 * LEN), lambda i: (i, 0, 0, 0)),
        pl.BlockSpec((block, cols), lambda i: (i, 0)),
    ]
    if emit_x:
        out_shape.append(jax.ShapeDtypeStruct((rows, width), BF))
        out_specs.append(pl.BlockSpec((block, width), lambda i: (i, 0)))
    return pl.pallas_call(
        functools.partial(attend_kernel, seqs, emit_x),
        grid=(rows // block,),
        in_specs=[
            SMEM_SPEC,
            pl.BlockSpec((block, width), lambda i: (i, 0)),
            fixed(table.shape),
            fixed(w_half.shape),
            fixed(bias_half.shape),
        ],
        out_specs=out_specs,
        out_shape=out_shape,
        compiler_params=params(40),
        name="attend",
    )(lengths, tokens, table, w_half, bias_half)


def normalize(value):
    centred = value - jnp.mean(value, axis=1, keepdims=True)
    inv_std = lax.rsqrt(jnp.mean(centred * centred, axis=1, keepdims=True) + NORM_EPS)
    return centred * inv_std, inv_std


def normalize_back(scaled, normed, inv_std):
    return inv_std * (
        scaled
        - jnp.mean(scaled, axis=1, keepdims=True)
        - normed * jnp.mean(scaled * normed, axis=1, keepdims=True)
    )


def gelu_pair(v):
    u = jnp.abs(v) * (0.3275911 / math.sqrt(2.0)) + 1.0
    t = 1.0 / u
    e = jnp.exp(v * v * -0.5)
    poly = 0.5 * 1.061405429
    for coef in (-1.453152027, 1.421413741, -0.284496736, 0.254829592):
        poly = poly * t + 0.5 * coef
    tail = poly * t * e
    cdf = jnp.where(v < 0.0, tail, 1.0 - tail)
    return v * cdf, cdf + v * e * (1.0 / math.sqrt(2.0 * math.pi))


def mlp_kernel(
    seqs, chunk,
    src_ref, len_ref, weight_ref, tok_ref, table_ref, ctx_own_ref, ctx_oth_ref, cot_ref,
    wo_own_ref, wo_oth_ref, bo_ref, ga_ref, sa_ref,
    wu_own_ref, wu_oth_ref, bu_own_ref, bu_oth_ref, wd_own_ref, wd_oth_ref, bd_ref, gm_ref, sm_ref,
    normed_ref, inv_ref, mid_ref, hid_own_ref, hid_oth_ref, dg_own_ref, dg_oth_ref,
    out_ref, ograd_ref, mgrad_ref, sums_ref,
):
    step = pl.program_id(0)
    first_seq = step * seqs
    start_x = add_table(tok_ref, table_ref, first_seq, seqs)
    mid_in = start_x + (mm(ctx_own_ref[...], wo_own_ref[...]) + mm(ctx_oth_ref[...], wo_oth_ref[...])) + bo_ref[...]
    normed, inv = normalize(mid_in)
    normed_ref[...] = normed
    inv_ref[...] = inv
    mid_x = normed * ga_ref[...] + sa_ref[...]
    mid_low = mid_x.astype(BF)
    mid_ref[...] = mid_low
    total = mid_x + bd_ref[...]
    for wu_ref, bu_ref, wd_ref, hid_ref, dg_ref in (
        (wu_own_ref, bu_own_ref, wd_own_ref, hid_own_ref, dg_own_ref),
        (wu_oth_ref, bu_oth_ref, wd_oth_ref, hid_oth_ref, dg_oth_ref),
    ):
        for c in range(0, wu_ref.shape[1], chunk):
            pre = mm(mid_low, wu_ref[:, c : c + chunk]) + bu_ref[:, c : c + chunk].astype(F32)
            hidden, slope = gelu_pair(pre)
            hidden = hidden.astype(BF)
            hid_ref[:, c : c + chunk] = hidden
            dg_ref[:, c : c + chunk] = slope.astype(BF)
            total = total + mm(hidden, wd_ref[c : c + chunk, :])
    normed2, inv2 = normalize(total)
    out_ref[...] = normed2 * gm_ref[...] + sm_ref[...]
    scales = []
    pos = lax.broadcasted_iota(jnp.int32, (LEN, 1), 0)
    for s in range(seqs):
        inside = (pos >= src_ref[first_seq + s]) & (pos < len_ref[first_seq + s])
        scales.append(jnp.where(inside, weight_ref[first_seq + s], 0.0))
    e = cot_ref[...].astype(F32) * jnp.concatenate(scales, axis=0)
    ograd = normalize_back(e * gm_ref[...], normed2, inv2)
    ograd_ref[...] = ograd
    mgrad = ograd.astype(BF)
    mgrad_ref[...] = mgrad
    part = jnp.stack([fold8(mgrad.astype(F32)), fold8(e * normed2), fold8(e)])

    @pl.when(step == 0)
    def _():
        sums_ref[...] = part

    @pl.when(step > 0)
    def _():
        sums_ref[...] += part


def mlp(src, lengths, weight, tokens, table, ctx_own, ctx_oth, cot, wo_own, wo_oth, bo, ga, sa,
        wu_own, wu_oth, bu_own, bu_oth, wd_own, wd_oth, bd, gm, sm):
    rows, width = tokens.shape
    seqs = 2
    block = seqs * LEN
    cols = ctx_own.shape[1]
    ff = wu_own.shape[1]
    row_block = lambda n: pl.BlockSpec((block, n), lambda i: (i, 0))
    resident = (wo_own, wo_oth, bo, ga, sa, wu_own, wu_oth, bu_own, bu_oth, wd_own, wd_oth, bd, gm, sm)
    sds = jax.ShapeDtypeStruct
    return pl.pallas_call(
        functools.partial(mlp_kernel, seqs, 512),
        grid=(rows // block,),
        in_specs=[SMEM_SPEC] * 3
        + [row_block(width), fixed(table.shape), row_block(cols), row_block(cols), row_block(width)]
        + [fixed(a.shape) for a in resident],
        out_specs=[
            row_block(width), row_block(1), row_block(width),
            row_block(ff), row_block(ff), row_block(ff), row_block(ff),
            row_block(width), row_block(width), row_block(width),
            fixed((3, 8, width)),
        ],
        out_shape=[
            sds((rows, width), F32), sds((rows, 1), F32), sds((rows, width), BF),
            sds((rows, ff), BF), sds((rows, ff), BF), sds((rows, ff), BF), sds((rows, ff), BF),
            sds((rows, width), F32), sds((rows, width), F32), sds((rows, width), BF),
            sds((3, 8, width), F32),
        ],
        compiler_params=params(56),
        name="mlp",
    )(src, lengths, weight, tokens, table, ctx_own, ctx_oth, cot, *resident)


def pre_kernel(mgrad_ref, wd_own_ref, wd_oth_ref, dg_own_ref, dg_oth_ref, pg_own_ref, pg_oth_ref, sum_own_ref, sum_oth_ref):
    for wd_ref, dg_ref, pg_ref, sum_ref in (
        (wd_oth_ref, dg_oth_ref, pg_oth_ref, sum_oth_ref),
        (wd_own_ref, dg_own_ref, pg_own_ref, sum_own_ref),
    ):
        pg = (mm(mgrad_ref[...], wd_ref[...], NT) * dg_ref[...].astype(F32)).astype(BF)
        pg_ref[...] = pg
        sum_ref[...] = fold8(pg.astype(F32))


def pre_grads(mgrad, wd_own, wd_oth, dg_own, dg_oth):
    rows, width = mgrad.shape
    ff = wd_own.shape[0]
    chunk = 256
    sds = jax.ShapeDtypeStruct
    wspec = pl.BlockSpec((chunk, width), lambda i: (i, 0))
    cspec = pl.BlockSpec((rows, chunk), lambda i: (0, i))
    sspec = pl.BlockSpec((8, chunk), lambda i: (0, i))
    return pl.pallas_call(
        pre_kernel,
        grid=(ff // chunk,),
        in_specs=[fixed(mgrad.shape), wspec, wspec, cspec, cspec],
        out_specs=[cspec, cspec, sspec, sspec],
        out_shape=[sds((rows, ff), BF), sds((rows, ff), BF), sds((8, ff), F32), sds((8, ff), F32)],
        compiler_params=params(40),
        name="pre_grads",
    )(mgrad, wd_own, wd_oth, dg_own, dg_oth)


def wgrad_kernel(groups, per_group, has_recv, lhs_ref, rhs_ref, *refs):
    out_ref = refs[-1]
    full = mm(lhs_ref[...], rhs_ref[...], TN)
    size = full.shape[0] // (groups * per_group)
    for g in range(groups):
        for k in range(per_group):
            first = (g * per_group + k) * size
            piece = full[first : first + size]
            if has_recv:
                piece = piece + refs[0][k, g].astype(F32)
            out_ref[k, g] = piece.astype(BF)


def wgrad(lhs, rhs, dp, plane, recv=None):
    rows, m = lhs.shape
    n = rhs.shape[1]
    outer = dp // plane
    steps = outer
    while (m // steps) % 128:
        steps //= 2
    groups = outer // steps
    size = m // dp
    spec = pl.BlockSpec((plane, groups, size, n), lambda i: (0, i, 0, 0))
    extra = [] if recv is None else [recv]
    return pl.pallas_call(
        functools.partial(wgrad_kernel, groups, plane, recv is not None),
        grid=(steps,),
        in_specs=[pl.BlockSpec((rows, m // steps), lambda i: (0, i)), fixed(rhs.shape)] + [spec] * len(extra),
        out_specs=spec,
        out_shape=jax.ShapeDtypeStruct((plane, outer, size, n), BF),
        compiler_params=params(40),
        name="wgrad",
    )(lhs, rhs, *extra)


def attn_wgrad_kernel(outer, plane, has_recv, x_ref, dqkv_ref, ctx_ref, agrad_ref, *refs):
    out_ref = refs[-1]

    def put(k, g, s, first, piece):
        last = first + piece.shape[0]
        if has_recv:
            piece = piece + refs[0][k, g, s, first:last, :].astype(F32)
        out_ref[k, g, s, first:last, :] = piece.astype(BF)

    cols = dqkv_ref.shape[2]
    size = x_ref.shape[1] // (outer * plane)
    for s in range(3):
        full = mm(x_ref[...], dqkv_ref[s], TN)
        for g in range(outer):
            for k in range(plane):
                first = (g * plane + k) * size
                put(k, g, s, 0, full[first : first + size])
    full = mm(ctx_ref[...], agrad_ref[...], TN)
    size = ctx_ref.shape[1] // (outer * plane)
    for g in range(outer):
        for k in range(plane):
            first = (g * plane + k) * size
            for c in range(2):
                put(k, g, 3, c * size, full[first : first + size, c * cols : (c + 1) * cols])


def attn_wgrad(x_low, dqkv, ctx, agrad, dp, plane, recv=None):
    size = x_low.shape[1] // dp
    cols = dqkv.shape[2]
    outer = dp // plane
    extra = [] if recv is None else [recv]
    return pl.pallas_call(
        functools.partial(attn_wgrad_kernel, outer, plane, recv is not None),
        in_specs=[VMEM_SPEC] * (4 + len(extra)),
        out_specs=VMEM_SPEC,
        out_shape=jax.ShapeDtypeStruct((plane, outer, 4, size, cols), BF),
        compiler_params=params(40),
        name="attn_wgrad",
    )(x_low, dqkv, ctx, agrad, *extra)


def mid_kernel(
    pg_own_ref, pg_oth_ref, ograd_ref, normed_ref, inv_ref, wu_own_ref, wu_oth_ref, wo_own_ref, wo_oth_ref, ga_ref,
    migrad_ref, agrad_ref, cg_own_ref, cg_oth_ref, sums_ref,
):
    step = pl.program_id(0)
    e = mm(pg_own_ref[...], wu_own_ref[...], NT) + mm(pg_oth_ref[...], wu_oth_ref[...], NT) + ograd_ref[...]
    normed = normed_ref[...]
    migrad = normalize_back(e * ga_ref[...], normed, inv_ref[...])
    migrad_ref[...] = migrad
    agrad = migrad.astype(BF)
    agrad_ref[...] = agrad
    cg_own_ref[...] = mm(agrad, wo_own_ref[...], NT).astype(BF)
    cg_oth_ref[...] = mm(agrad, wo_oth_ref[...], NT).astype(BF)
    part = jnp.stack([fold8(e * normed), fold8(e), fold8(agrad.astype(F32))])

    @pl.when(step == 0)
    def _():
        sums_ref[...] = part

    @pl.when(step > 0)
    def _():
        sums_ref[...] += part


def mid_grads(pg_own, pg_oth, ograd, normed, inv, wu_own, wu_oth, wo_own, wo_oth, ga):
    rows, width = ograd.shape
    ff = pg_own.shape[1]
    cols = wo_own.shape[0]
    block = 256
    row_block = lambda n: pl.BlockSpec((block, n), lambda i: (i, 0))
    resident = (wu_own, wu_oth, wo_own, wo_oth, ga)
    sds = jax.ShapeDtypeStruct
    return pl.pallas_call(
        mid_kernel,
        grid=(rows // block,),
        in_specs=[row_block(ff), row_block(ff), row_block(width), row_block(width), row_block(1)]
        + [fixed(a.shape) for a in resident],
        out_specs=[row_block(width), row_block(width), row_block(cols), row_block(cols), fixed((3, 8, width))],
        out_shape=[
            sds((rows, width), F32), sds((rows, width), BF), sds((rows, cols), BF), sds((rows, cols), BF),
            sds((3, 8, width), F32),
        ],
        compiler_params=params(40),
        name="mid_grads",
    )(pg_own, pg_oth, ograd, normed, inv, *resident)


def attend_back_kernel(seqs, qkv_ref, prob_ref, cg_ref, dqkv_ref, sums_ref):
    scale_a, scale_b = half_masks(LEN, HD**-0.5)
    one_a, one_b = half_masks(LEN)
    sums = [[], []]
    for j in range(cg_ref.shape[1] // PAIR):
        cols = slice(j * PAIR, (j + 1) * PAIR)
        col_sums = [0.0, 0.0]
        for s in range(seqs):
            rows = slice(s * LEN, (s + 1) * LEN)
            q2, k2, v2, g2 = qkv_ref[0, rows, cols], qkv_ref[1, rows, cols], qkv_ref[2, rows, cols], cg_ref[rows, cols]
            qcat = jnp.concatenate([q2 * scale_a, q2 * scale_b], axis=0)
            kcat = jnp.concatenate([k2 * scale_a, k2 * scale_b], axis=0)
            vcat = jnp.concatenate([v2 * one_a, v2 * one_b], axis=0)
            gcat = jnp.concatenate([g2 * one_a, g2 * one_b], axis=0)
            probs = prob_ref[s, j]
            dprobs = mm(g2, vcat, NT)
            tall, flat = [], []
            for h in range(2):
                p = probs[:, h * LEN : (h + 1) * LEN]
                dp = dprobs[:, h * LEN : (h + 1) * LEN]
                ds = (p * (dp - jnp.sum(p * dp, axis=1, keepdims=True))).astype(BF)
                flat.append(ds)
                tall.append(p.astype(BF))
            dq = mm(jnp.concatenate(flat, axis=1), kcat).astype(BF)
            dk = mm(jnp.concatenate(flat, axis=0), qcat, TN).astype(BF)
            dv = mm(jnp.concatenate(tall, axis=0), gcat, TN).astype(BF)
            dqkv_ref[0, rows, cols] = dq
            dqkv_ref[1, rows, cols] = dk
            dqkv_ref[2, rows, cols] = dv
            col_sums[0] += fold8(dq.astype(F32))
            col_sums[1] += fold8(dv.astype(F32))
        sums[0].append(col_sums[0])
        sums[1].append(col_sums[1])
    part = jnp.stack([jnp.concatenate(sums[0], axis=1), jnp.concatenate(sums[1], axis=1)])
    step = pl.program_id(0)

    @pl.when(step == 0)
    def _():
        sums_ref[...] = part

    @pl.when(step > 0)
    def _():
        sums_ref[...] += part


def attend_back(qkv, probs, cgrad):
    rows, cols = cgrad.shape
    seqs = 2
    block = seqs * LEN
    pairs = cols // PAIR
    sds = jax.ShapeDtypeStruct
    spec3 = pl.BlockSpec((3, block, cols), lambda i: (0, i, 0))
    return pl.pallas_call(
        functools.partial(attend_back_kernel, seqs),
        grid=(rows // block,),
        in_specs=[
            spec3,
            pl.BlockSpec((seqs, pairs, LEN, 2 * LEN), lambda i: (i, 0, 0, 0)),
            pl.BlockSpec((block, cols), lambda i: (i, 0)),
        ],
        out_specs=[spec3, fixed((2, 8, cols))],
        out_shape=[sds((3, rows, cols), BF), sds((2, 8, cols), F32)],
        compiler_params=params(40),
        name="attend_back",
    )(qkv, probs, cgrad)


def token_kernel(own_ref, oth_ref, migrad_ref, w_own_ref, w_oth_ref, out_ref):
    total = migrad_ref[...]
    for d_ref, w_ref in ((own_ref, w_own_ref), (oth_ref, w_oth_ref)):
        for s in range(3):
            total = total + mm(d_ref[s], w_ref[s], NT)
    out_ref[...] = total


def token_grads(dqkv_own, dqkv_oth, migrad, w_own, w_oth):
    rows, width = migrad.shape
    cols = dqkv_own.shape[2]
    block = 256
    spec3 = pl.BlockSpec((3, block, cols), lambda i: (0, i, 0))
    row_spec = pl.BlockSpec((block, width), lambda i: (i, 0))
    return pl.pallas_call(
        token_kernel,
        grid=(rows // block,),
        in_specs=[spec3, spec3, row_spec, fixed(w_own.shape), fixed(w_oth.shape)],
        out_specs=row_spec,
        out_shape=jax.ShapeDtypeStruct((rows, width), F32),
        compiler_params=params(40),
        name="token_grads",
    )(dqkv_own, dqkv_oth, migrad, w_own, w_oth)


def per_device(
    tokens, timesteps, src_len, tgt_len, sample_weight, w_qkv, bias_qv, w_out, bias_out, gain_attn, shift_attn,
    w_up, bias_up, w_down, bias_down, gain_mlp, shift_mlp, cotangent,
):
    rows, width = tokens.shape
    dp = lax.axis_size("dp")
    mp_index = lax.axis_index("mp")
    seqs = rows // LEN
    cols = bias_qv.shape[1]
    ff = bias_up.shape[0]
    plane = 4

    def swap(value):
        return lax.ppermute(value, "mp", [(0, 1), (1, 0)])

    def mine(value):
        return lax.dynamic_slice_in_dim(value, mp_index * seqs, seqs)

    table = time_table(mine(timesteps), width)
    src = mine(src_len)
    lengths = src + mine(tgt_len)
    weight = mine(sample_weight)
    qkv_oth_w = swap(w_qkv)
    biases = jnp.concatenate([bias_qv.reshape(-1), bias_up])
    biases_oth = swap(biases)
    bqv_oth, bu_oth = biases_oth[: 2 * cols].reshape(2, cols), biases_oth[2 * cols :].reshape(1, ff)
    wo_oth = swap(w_out)
    wu_oth = swap(w_up)
    wd_oth = swap(w_down)
    row = lambda vec: vec.reshape(1, -1)

    qkv_own, prob_own, ctx_own, x_low = attend(tokens, table, lengths, w_qkv, bias_qv.astype(F32), True)
    qkv_oth, prob_oth, ctx_oth = attend(tokens, table, lengths, qkv_oth_w, bqv_oth.astype(F32), False)
    (normed, inv, mid_low, hid_own, hid_oth, dg_own, dg_oth, layer_out, ograd, mgrad, sums_mlp) = mlp(
        src, lengths, weight, tokens, table, ctx_own, ctx_oth, cotangent, w_out, wo_oth, row(bias_out),
        row(gain_attn), row(shift_attn), w_up, wu_oth, row(bias_up), bu_oth, w_down, wd_oth, row(bias_down),
        row(gain_mlp), row(shift_mlp),
    )
    down_recv = swap(wgrad(hid_oth, mgrad, dp, plane))
    pg_own, pg_oth, sum_up_own, sum_up_oth = pre_grads(mgrad, w_down, wd_oth, dg_own, dg_oth)
    down_part = wgrad(hid_own, mgrad, dp, plane, down_recv)
    up_recv = swap(wgrad(mid_low, pg_oth, dp, plane))
    migrad, agrad, cg_own, cg_oth, sums_mid = mid_grads(
        pg_own, pg_oth, ograd, normed, inv, w_up, wu_oth, w_out, wo_oth, row(gain_attn)
    )
    up_part = wgrad(mid_low, pg_own, dp, plane, up_recv)
    dqkv_oth, sum_qv_oth = attend_back(qkv_oth, prob_oth, cg_oth)
    attn_recv = swap(attn_wgrad(x_low, dqkv_oth, ctx_oth, agrad, dp, plane))
    dqkv_own, sum_qv_own = attend_back(qkv_own, prob_own, cg_own)
    attn_part = attn_wgrad(x_low, dqkv_own, ctx_own, agrad, dp, plane, attn_recv)
    tokens_grad = token_grads(dqkv_own, dqkv_oth, migrad, w_qkv, qkv_oth_w)

    in_plane = [[base + k for k in range(plane)] for base in range(0, dp, plane)]
    across = [[base * plane + k for base in range(dp // plane)] for k in range(plane)]

    def scatter(part):
        part = lax.psum_scatter(part, "dp", scatter_dimension=0, axis_index_groups=in_plane)
        return lax.psum_scatter(part, "dp", scatter_dimension=0, axis_index_groups=across).astype(F32)

    grad_w_down = scatter(down_part)
    grad_w_up = scatter(up_part)
    attn_out = scatter(attn_part)
    grad_w_qkv = attn_out[:3]
    half = attn_out.shape[1] // 2
    grad_w_out = jnp.concatenate([attn_out[3, :half], attn_out[3, half:]], axis=1)

    fold = lambda value: jnp.sum(value, axis=-2)
    shared = jnp.concatenate([fold(sums_mid), fold(sums_mlp)]).reshape(-1)
    oth = jnp.concatenate([fold(sum_up_oth), fold(sum_qv_oth).reshape(-1)])
    own = jnp.concatenate([fold(sum_up_own), fold(sum_qv_own).reshape(-1)])
    vec = jnp.concatenate([shared, own]) + swap(jnp.concatenate([shared, oth]))
    bit = 1
    while bit < dp:
        vec = vec + lax.ppermute(vec, "dp", [(i, i ^ bit) for i in range(dp)])
        bit *= 2
    shared = vec[: 6 * width].reshape(6, width)
    grad_rows = jnp.concatenate([shared[0:2], shared[3:6]])
    grad_bias_out = shared[2]
    grad_bias_up = vec[6 * width : 6 * width + ff]
    grad_bias_qv = vec[6 * width + ff :].reshape(2, cols)
    return (
        layer_out, tokens_grad, grad_w_qkv, grad_w_out, grad_w_up, grad_w_down,
        grad_bias_qv, grad_bias_up, grad_bias_out, grad_rows,
    )


def solution(mesh):
    in_specs = (
        P(("dp", "mp"), None), P("dp"), P("dp"), P("dp"), P("dp"),
        P(None, None, "mp"), P(None, "mp"), P("mp", None), P(), P(), P(),
        P(None, "mp"), P("mp"), P("mp", None), P(), P(), P(), P(("dp", "mp"), None),
    )
    out_specs = (
        P(("dp", "mp"), None), P(("dp", "mp"), None), P(None, "dp", "mp"), P(("mp", "dp"), None),
        P("dp", "mp"), P(("mp", "dp"), None), P(None, "mp"), P("mp"), P(), P(),
    )
    return jax.shard_map(per_device, mesh=mesh, in_specs=in_specs, out_specs=out_specs, check_vma=False)
```

time: 949 us -> 339 us (0.36)
  waiting for transfers between devices: 622 us -> 138 us
  matrix products: 143 us -> 0 us
  Pallas kernels: 0 us -> 115 us
  blocking collectives: 42.4 us -> 0 us
  other arithmetic: 40.1 us -> 9.22 us
  local copies, waits for them, and re-layouts: 80.4 us -> 51.7 us
    reduce_scatter x7 -> x3, waiting for transfers between devices: 468 us -> 63.5 us  [scatter(): lax.psum_scatter(part, 'dp', scatter_dimension=0, axis_index_groups=across)]
    dot_general x18 -> x0, matrix products: 143 us -> none  [the longest x1 34 us: per_device(): jnp.dot(mid_all, up_w, preferred_element_type=jnp.float32) + up_bias]
    pallas_call x0 -> x14, Pallas kernels: none -> 115 us  [the longest x1 33.2 us: mlp(): pl.pallas_call(functools.partial(mlp_kernel, seqs, 512), grid=(rows // bl...]
    all_gather x4 -> x0, waiting for transfers between devices: 54.8 us -> none  [the longest x1 14.7 us: per_device(): x_all = lax.all_gather(x_low, 'mp', axis=0, tiled=True)]
    psum x1 -> x0, blocking collectives: 42.4 us -> none  [per_device(): lax.psum((row_terms, out_bias_term, qv_full, up_full), ('dp', 'mp'))]
    unnamed x13 -> x9, waiting for transfers between devices: 98.9 us -> 57.8 us
    reduce_sum x11 -> x6, other arithmetic: 26.7 us -> 0.14 us  [per_device(): fold = lambda value: jnp.sum(value, axis=-2)]
    another operation x14 -> x0, local copies, waits for them, and re-layouts: 19.1 us -> none  [the longest x6 19 us: attend_backward(): jnp.stack([grad_queries.reshape(flat_shape), grad_keys.reshape(flat_shape...]
  transfers between devices with their start and end apart: 12 -> 19, of which waited for: 12 -> 12; matrix products, arithmetic and copies ran while one was open for 5% -> 6% of each run, Pallas kernels for 0% -> 13%
where the time goes in v1:
time: 339 us; the launch traced here: 338 us
  waiting for transfers between devices  138 us (41%)
  Pallas kernels  115 us (34%)
  local copies, waits for them, and re-layouts  51.7 us (15%)
  between operations  14.6 us (4%)
  starting transfers between devices  9.57 us (3%)
  other arithmetic  9.22 us (3%)
    reduce_scatter x3, waiting for transfers between devices, scatter(): lax.psum_scatter(part, 'dp', scatter_dimension=0, axis_index_groups=across)  63.5 us
    unnamed x9, waiting for transfers between devices  57.8 us
    unnamed x92, local copies, waits for them, and re-layouts  37.6 us
    pallas_call x1, Pallas kernels, mlp(): pl.pallas_call(functools.partial(mlp_kernel, seqs, 512), grid=(rows // bl...  33.2 us
    pallas_call x2, Pallas kernels, attend_back(): pl.pallas_call(functools.partial(attend_back_kernel, seqs), grid=(rows //...  17.4 us
    pallas_call x1, Pallas kernels, mid_grads(): pl.pallas_call(mid_kernel, grid=(rows // block,), in_specs=[row_block(ff)...  14.7 us
    pallas_call x4, Pallas kernels, wgrad(): pl.pallas_call(functools.partial(wgrad_kernel, groups, plane, recv is not...  14.4 us
    pallas_call x2, Pallas kernels, attend(): pl.pallas_call(functools.partial(attend_kernel, seqs, emit_x), grid=(rows...  12.5 us
  transfers between devices with their start and end apart: 19, of which 12 were waited for; matrix products, arithmetic and copies ran while one was open for 6% of the time, Pallas kernels for 13%

profile of v1, /device:TPU:0, one launch (start us, length us, event | category | flops | bytes accessed | tf_op | source)
XLA Modules:
  0.0 337.8 jit_solution(16757557614553273322)
XLA Ops:
  11.0 1.3 dynamic-slice_add_fusion
  13.0 1.3 reshape.118.bu_own_ref
  14.3 1.3 dynamic_slice.14.weight_ref
  15.6 1.3 reshape.116.ga_ref
  16.9 1.3 reshape.115.bo_ref
  18.1 1.3 reshape.117.sa_ref
  19.4 1.3 reshape.120.bd_ref
  20.7 1.3 reshape.121.gm_ref
  22.0 1.3 reshape.122.sm_ref
  23.2 1.4 copy-done.2
  24.6 1.5 copy-done.17
  26.1 6.2 %attend.2 = (bf16[3,1024,384]{2,1,0:T(8,128)(2,1)S(1)}, f32[8,3,128,256]{3,2,1,0:T(8,128)S(1)}, bf16[1024,384]{1,0:T(8,128)(2,1)S(1)}, bf16[1024,768]{1,0:T(8,128)(2,1)S(1)}) custom-call(s32[8]{0:T(128)S(1)} %get-tuple-element.72.len_ref, bf16[1024,768]{1,0:T(8,128)(2,1)S(1)} %copy-done.2, f32[8,768]{1,0:T(8,128)S(1)} %pad_maximum_fusion.3.table_ref, ...), custom_call_target="tpu_custom_call" | custom-call | tf_op jit(solution)/shard_map/attend/pallas_call | solution.py:124
  32.4 1.1 copy-done.22
  34.4 1.6 copy-done.31
  36.0 1.5 copy-done.37
  38.1 6.3 %attend.3 = (bf16[3,1024,384]{2,1,0:T(8,128)(2,1)S(1)}, f32[8,3,128,256]{3,2,1,0:T(8,128)S(1)}, bf16[1024,384]{1,0:T(8,128)(2,1)S(1)}) custom-call(s32[8]{0:T(128)S(1)} %get-tuple-element.72.len_ref, bf16[1024,768]{1,0:T(8,128)(2,1)S(1)} %copy-done.3, f32[8,768]{1,0:T(8,128)S(1)} %pad_maximum_fusion.3.table_ref, ...), custom_call_target="tpu_custom_call" | custom-call | tf_op jit(solution)/shard_map/attend/pallas_call | solution.py:124
  45.3 1.7 copy-done.33
  47.1 1.4 copy-done.39
  48.5 33.2 %mlp.1 = (f32[1024,768]{1,0:T(8,128)}, f32[1024,1]{1,0:T(8,128)}, bf16[1024,768]{1,0:T(8,128)(2,1)}, bf16[1024,1536]{1,0:T(8,128)(2,1)}, bf16[1024,1536]{1,0:T(8...) custom-call(s32[8]{0:T(128)} %get-tuple-element.73.src_ref, ...), custom_call_target="tpu_custom_call" | custom-call | tf_op jit(solution)/shard_map/mlp/pallas_call | solution.py:230
  81.7 1.4 copy-done
  83.2 8.9 %pre_grads.1 = (bf16[1024,1536]{1,0:T(8,128)(2,1)S(1)}, bf16[1024,1536]{1,0:T(8,128)(2,1)S(1)}, f32[8,1536]{1,0:T(8,128)S(1)}, f32[8,1536]{1,0:T(8,128)S(1)}) custom-call(bf16[1024,768]{1,0:T(8,128)(2,1)S(1)} %copy-done, bf16[1536,768]{1,0:T(8,128)(2,1)S(1)} %copy-done.9, bf16[1536,768]{1,0:T(8,128)(2,1)} %collective-permute-done.4.wd_oth_ref, ...), custom_call_target="tpu_custom_call" | custom-call | tf_op jit(solution)/shard_map/pre_grads/pallas_call | solution.py:271
  92.1 1.7 copy-done.4
  93.7 1.6 copy-done.6
  95.4 14.7 %mid_grads.1 = (f32[1024,768]{1,0:T(8,128)S(1)}, bf16[1024,768]{1,0:T(8,128)(2,1)S(1)}, bf16[1024,384]{1,0:T(8,128)(2,1)S(1)}, bf16[1024,384]{1,0:T(8,128)(2,1)S(1)}, f32[3,8,768]{2,1,0:T(8,128)S(1)}) custom-call(bf16[1024,1536]{1,0:T(8,128)(2,1)} %copy-done.6, bf16[1024,1536]{1,0:T(8,128)(2,1)} %copy-done.4, f32[1024,768]{1,0:T(8,128)} %get-tuple-element.51.ograd_ref, ...), custom_call_target="tpu_custom_call" | custom-call | tf_op jit(solution)/shard_map/mid_grads/pallas_call | solution.py:390
  110.1 1.7 copy-done.26
  111.8 8.8 %attend_back.3 = (bf16[3,1024,384]{2,1,0:T(8,128)(2,1)S(1)}, f32[2,8,384]{2,1,0:T(8,128)S(1)}) custom-call(bf16[3,1024,384]{2,1,0:T(8,128)(2,1)S(1)} %copy-done.40, f32[8,3,128,256]{3,2,1,0:T(8,128)S(1)} %copy-done.34, bf16[1024,384]{1,0:T(8,128)(2,1)S(1)} %get-tuple-element.58.cg_ref), custom_call_target="tpu_custom_call" | custom-call | tf_op jit(solution)/shard_map/attend_back/pallas_call | solution.py:457
  120.6 3.3 attn_wgrad.2
  124.1 8.6 %attend_back.2 = (bf16[3,1024,384]{2,1,0:T(8,128)(2,1)S(1)}, f32[2,8,384]{2,1,0:T(8,128)S(1)}) custom-call(bf16[3,1024,384]{2,1,0:T(8,128)(2,1)S(1)} %copy-done.38, f32[8,3,128,256]{3,2,1,0:T(8,128)S(1)} %copy-done.32, bf16[1024,384]{1,0:T(8,128)(2,1)S(1)} %get-tuple-element.54.cg_ref), custom_call_target="tpu_custom_call" | custom-call | tf_op jit(solution)/shard_map/attend_back/pallas_call | solution.py:457
  132.7 3.3 attn_wgrad.3
  136.0 1.4 copy-done.12
  137.4 1.4 copy-done.15
  138.9 1.3 copy-done.1
  140.2 1.9 copy-done.28
  142.1 3.8 %wgrad.6 = bf16[4,4,96,768]{3,2,1,0:T(8,128)(2,1)S(1)} custom-call(bf16[1024,1536]{1,0:T(8,128)(2,1)S(1)} %copy-done.28, bf16[1024,768]{1,0:T(8,128)(2,1)S(1)} %copy-done.1), custom_call_target="tpu_custom_call" | custom-call | tf_op jit(solution)/shard_map/wgrad/pallas_call | solution.py:306
  146.5 4.2 %collective-permute-done.7.refs_0_ = bf16[4,4,96,768]{3,2,1,0:T(8,128)(2,1)S(1)} collective-permute-done((bf16[4,4,96,768]{3,2,1,0:T(8,128)(2,1)S(1)}, bf16[4,4,96,768]{3,2,1,0:T(8,128)(2,1)S(1)}, u32[]{:S(2)}, u32[]{:S(2)}) %collective-permute-start.7) | collective-permute-done | bytes 2359328 | tf_op jit(solution)/shard_map/ppermute | solution.py:510
  150.6 4.0 %wgrad.7 = bf16[4,4,96,768]{3,2,1,0:T(8,128)(2,1)S(1)} custom-call(bf16[1024,1536]{1,0:T(8,128)(2,1)S(1)} %copy-done.35, bf16[1024,768]{1,0:T(8,128)(2,1)S(1)} %copy-done.1, bf16[4,4,96,768]{3,2,1,0:T(8,128)(2,1)S(1)} %collective-permute-done.7.refs_0_), custom_call_target="tpu_custom_call" | custom-call | tf_op jit(solution)/shard_map/wgrad/pallas_call | solution.py:306
  154.7 1.4 copy-done.16
  156.1 1.4 copy-done.21
  157.6 2.0 copy-done.5
  159.5 3.2 wgrad.4
  163.0 4.3 %collective-permute-done.6.refs_0_ = bf16[4,4,48,1536]{3,2,1,0:T(8,128)(2,1)S(1)} collective-permute-done((bf16[4,4,48,1536]{3,2,1,0:T(8,128)(2,1)S(1)}, bf16[4,4,48,1536]{3,2,1,0:T(8,128)(2,1)S(1)}, u32[]{:S(2)}, u32[]{:S(2)}) %collective-permute-start.6) | collective-permute-done | bytes 2359328 | tf_op jit(solution)/shard_map/ppermute | solution.py:510
  167.3 3.3 wgrad.5
  170.6 1.4 copy-done.14
  172.2 6.9 %reduce-scatter.19.cloned.1.call-done = bf16[1,4,4,48,384]{4,3,2,1,0:T(8,128)(2,1)} async-done(((bf16[4,4,4,48,384]{4,3,2,1,0:T(8,128)(2,1)}), bf16[1,4,4,48,384]{4,3,2,1,0:T(8,128)(2,1)}) %reduce-scatter.19.cloned.1.call-update) | async-done | bytes 589840
  179.1 40.4 %reduce-scatter.23.cloned.1.call-done = bf16[1,4,96,768]{3,2,1,0:T(8,128)(2,1)} async-done(((bf16[4,4,96,768]{3,2,1,0:T(8,128)(2,1)}), bf16[1,4,96,768]{3,2,1,0:T(8,128)(2,1)}) %reduce-scatter.23.cloned.1.call-update) | async-done | bytes 589840
  219.9 1.1 collective-permute-done.8
  221.1 1.4 collective-permute-start.9
  222.5 2.4 collective-permute-done.9
  224.9 1.4 collective-permute-start.10
  226.4 2.4 collective-permute-done.10
  228.8 1.5 collective-permute-start.11
  230.3 2.4 collective-permute-done.11
  232.7 2.4 collective-permute-start.12
  235.1 1.8 copy-done.13
  236.9 1.6 copy-done.18
  238.5 1.6 copy-done.20
  240.1 1.9 copy-done.27
  242.0 7.0 %token_grads.1 = f32[1024,768]{1,0:T(8,128)} custom-call(bf16[3,1024,384]{2,1,0:T(8,128)(2,1)S(1)} %copy-done.13, bf16[3,1024,384]{2,1,0:T(8,128)(2,1)S(1)} %copy-done.11, f32[1024,768]{1,0:T(8,128)S(1)} %copy-done.27, bf16[3,768,384]{2,1,0:T(8,128)(2,1)S(1)} %copy-done.18, bf16[3,768,384]{2,1,0:T(8,128)(2,1)S(1)} %copy-done.20), custom_call_target="tpu_custom_call" | custom-call | tf_op jit(solution)/shard_map/token_grads/pallas_call | solution.py:486
  249.6 10.4 %reduce-scatter.21.cloned.1.call-done = bf16[1,4,48,1536]{3,2,1,0:T(8,128)(2,1)} async-done(((bf16[4,4,48,1536]{3,2,1,0:T(8,128)(2,1)}), bf16[1,4,48,1536]{3,2,1,0:T(8,128)(2,1)}) %reduce-scatter.21.cloned.1.call-update) | async-done | bytes 589840
  261.9 22.3 %reduce-scatter.13.cloned.1.call-done = bf16[1,4,48,384]{3,2,1,0:T(8,128)(2,1)} async-done(((bf16[4,4,48,384]{3,2,1,0:T(8,128)(2,1)}), bf16[1,4,48,384]{3,2,1,0:T(8,128)(2,1)}) %reduce-scatter.13.cloned.1.call-update) | async-done | bytes 147472 | tf_op jit(solution)/shard_map/reduce_scatter | solution.py:554
  286.5 20.2 %reduce-scatter.17.cloned.1.call-done = bf16[1,96,768]{2,1,0:T(8,128)(2,1)} async-done(((bf16[4,96,768]{2,1,0:T(8,128)(2,1)}), bf16[1,96,768]{2,1,0:T(8,128)(2,1)}) %reduce-scatter.17.cloned.1.call-update) | async-done | bytes 147472 | tf_op jit(solution)/shard_map/reduce_scatter | solution.py:554
  306.8 1.6 bitcast_convert_fusion
  308.4 20.9 %reduce-scatter.15.cloned.1.call-done = bf16[1,48,1536]{2,1,0:T(8,128)(2,1)} async-done(((bf16[4,48,1536]{2,1,0:T(8,128)(2,1)}), bf16[1,48,1536]{2,1,0:T(8,128)(2,1)}) %reduce-scatter.15.cloned.1.call-update) | async-done | bytes 147472 | tf_op jit(solution)/shard_map/reduce_scatter | solution.py:554
  329.3 1.6 bitcast_convert_fusion.1
  (135 shorter events, 13.3 us)
Async XLA Ops:
  7.2 171.9 %reduce-scatter.19.cloned.1.call-start = ((), (), s32[]{:S(2)}) async-start(), calls=%async_computation.9 | async-start | bytes 2949120
  7.2 41.2 %collective-permute-start.3 = (bf16[768,1536]{1,0:T(8,128)(2,1)}, bf16[768,1536]{1,0:T(8,128)(2,1)}, u32[]{:S(2)}, u32[]{:S(2)}) collective-permute-start(bf16[768,1536]{1,0:T(8,128)(2,1)} %wu_own_ref.3), channel_id=1, source_target_pairs={{0,1},{1,0},{2,3},{3,2},{4,5},{5,4},{6,7},{7,6},{8,9},{9,8},{10,11... | collective-permute-start | bytes 7077896 | tf_op jit(solution)/shard_map/ppermute | solution.py:510
  7.7 40.7 %collective-permute-start.4 = (bf16[1536,768]{1,0:T(8,128)(2,1)}, bf16[1536,768]{1,0:T(8,128)(2,1)}, u32[]{:S(2)}, u32[]{:S(2)}) collective-permute-start(bf16[1536,768]{1,0:T(8,128)(2,1)} %wd_own_ref.3), channel_id=1, source_target_pairs={{0,1},{1,0},{2,3},{3,2},{4,5},{5,4},{6,7},{7,6},{8,9},{9,8},{10,11... | collective-permute-start | bytes 7077896 | tf_op jit(solution)/shard_map/ppermute | solution.py:510
  7.8 30.3 %collective-permute-start = (bf16[3,768,384]{2,1,0:T(8,128)(2,1)}, bf16[3,768,384]{2,1,0:T(8,128)(2,1)S(1)}, u32[]{:S(2)}, u32[]{:S(2)}) collective-permute-start(bf16[3,768,384]{2,1,0:T(8,128)(2,1)} %w_own_ref.1), channel_id=1, source_target_pairs={{0,1},{1,0},{2,3},{3,2},{4,5},{5,4},{6,7},{7,6},{8,9},{9,8},{10,11... | collective-permute-start | bytes 5308424 | tf_op jit(solution)/shard_map/ppermute | solution.py:510
  9.6 27.9 %collective-permute-start.1 = (bf16[2304]{0:T(1024)(128)(2,1)S(1)}, bf16[2304]{0:T(1024)(128)(2,1)S(1)}, u32[]{:S(2)}, u32[]{:S(2)}) collective-permute-start(bf16[2304]{0:T(1024)(128)(2,1)S(1)} %pad_maximum_fusion.6), channel_id=1, source_target_pairs={{0,1},{1,0},{2,3},{3,2},{4,5},{5,4},{6,7},{7,6},{8,9},{9,8},{10,11... | collective-permute-start | bytes 13832 | tf_op jit(solution)/shard_map/ppermute | solution.py:510
  9.7 38.7 %collective-permute-start.2 = (bf16[384,768]{1,0:T(8,128)(2,1)}, bf16[384,768]{1,0:T(8,128)(2,1)}, u32[]{:S(2)}, u32[]{:S(2)}) collective-permute-start(bf16[384,768]{1,0:T(8,128)(2,1)} %wo_own_ref.3), channel_id=1, source_target_pairs={{0,1},{1,0},{2,3},{3,2},{4,5},{5,4},{6,7},{7,6},{8,9},{9,8},{10,11... | collective-permute-start | bytes 1769480 | tf_op jit(solution)/shard_map/ppermute | solution.py:510
  11.0 33.4 %copy-start.42 = (f32[8,768]{1,0:T(8,128)}, f32[8,768]{1,0:T(8,128)S(1)}, u32[]{:S(2)}) copy-start(f32[8,768]{1,0:T(8,128)S(1)} %pad_maximum_fusion.3.table_ref) | copy-start | bytes 73732
  12.3 32.1 %copy-start.44 = (s32[8]{0:T(128)}, s32[8]{0:T(128)S(1)}, u32[]{:S(2)}) copy-start(s32[8]{0:T(128)S(1)} %get-tuple-element.72.len_ref) | copy-start | bytes 100
  23.2 1.4 copy-start.2
  24.6 1.5 copy-start.17
  26.1 12.0 %copy-start.3 = (bf16[1024,768]{1,0:T(8,128)(2,1)S(1)}, bf16[1024,768]{1,0:T(8,128)(2,1)}, u32[]{:S(2)}) copy-start(bf16[1024,768]{1,0:T(8,128)(2,1)} %tok_ref.5) | copy-start | bytes 4718596
  32.4 1.2 copy-start.22
  34.4 1.6 copy-start.31
  36.0 1.5 copy-start.37
  38.1 43.6 %copy-start.19 = (bf16[3,768,384]{2,1,0:T(8,128)(2,1)}, bf16[3,768,384]{2,1,0:T(8,128)(2,1)S(1)}, u32[]{:S(2)}) copy-start(bf16[3,768,384]{2,1,0:T(8,128)(2,1)S(1)} %collective-permute-done.w_ref.w_oth_ref) | copy-start | bytes 5308420
  44.4 0.9 copy-start.24
  45.3 1.7 copy-start.33
  47.1 1.4 copy-start.39
  48.5 33.2 %copy-start.9 = (bf16[1536,768]{1,0:T(8,128)(2,1)S(1)}, bf16[1536,768]{1,0:T(8,128)(2,1)}, u32[]{:S(2)}) copy-start(bf16[1536,768]{1,0:T(8,128)(2,1)} %wd_own_ref.3) | copy-start | bytes 7077892
  81.7 1.4 copy-start
  83.1 12.2 %copy-start.8 = (bf16[768,1536]{1,0:T(8,128)(2,1)S(1)}, bf16[768,1536]{1,0:T(8,128)(2,1)}, u32[]{:S(2)}) copy-start(bf16[768,1536]{1,0:T(8,128)(2,1)} %wu_own_ref.3) | copy-start | bytes 7077892
  83.1 12.2 %copy-start.36 = (bf16[384,768]{1,0:T(8,128)(2,1)S(1)}, bf16[384,768]{1,0:T(8,128)(2,1)}, u32[]{:S(2)}) copy-start(bf16[384,768]{1,0:T(8,128)(2,1)} %wo_own_ref.3) | copy-start | bytes 1769476
  83.1 12.2 %copy-start.41 = (f32[1024,1]{1,0:T(8,128)S(1)}, f32[1024,1]{1,0:T(8,128)}, u32[]{:S(2)}) copy-start(f32[1024,1]{1,0:T(8,128)} %get-tuple-element.53.inv_ref) | copy-start | bytes 12292
  83.1 12.2 %copy-start.43 = (f32[1,768]{1,0:T(1,128)S(1)}, f32[1,768]{1,0:T(1,128)}, u32[]{:S(2)}) copy-start(f32[1,768]{1,0:T(1,128)} %reshape.116.ga_ref) | copy-start | bytes 9220
  92.1 1.7 copy-start.4
  93.7 1.6 copy-start.6
  95.4 16.4 %copy-start.34 = (f32[8,3,128,256]{3,2,1,0:T(8,128)S(1)}, f32[8,3,128,256]{3,2,1,0:T(8,128)}, u32[]{:S(2)}) copy-start(f32[8,3,128,256]{3,2,1,0:T(8,128)} %copy-done.33) | copy-start | bytes 9437188
  95.4 16.4 %copy-start.40 = (bf16[3,1024,384]{2,1,0:T(8,128)(2,1)S(1)}, bf16[3,1024,384]{2,1,0:T(8,128)(2,1)}, u32[]{:S(2)}) copy-start(bf16[3,1024,384]{2,1,0:T(8,128)(2,1)} %copy-done.39) | copy-start | bytes 7077892
  110.1 1.7 copy-start.26
  111.8 8.8 %copy-start.23 = (bf16[1024,768]{1,0:T(8,128)(2,1)S(1)}, bf16[1024,768]{1,0:T(8,128)(2,1)}, u32[]{:S(2)}) copy-start(bf16[1024,768]{1,0:T(8,128)(2,1)} %copy-done.22) | copy-start | bytes 4718596
  111.8 8.8 %copy-start.25 = (bf16[1024,384]{1,0:T(8,128)(2,1)S(1)}, bf16[1024,384]{1,0:T(8,128)(2,1)}, u32[]{:S(2)}) copy-start(bf16[1024,384]{1,0:T(8,128)(2,1)} %copy-done.24) | copy-start | bytes 2359300
  120.6 3.3 copy-start.10
  120.6 3.5 %copy-start.32 = (f32[8,3,128,256]{3,2,1,0:T(8,128)S(1)}, f32[8,3,128,256]{3,2,1,0:T(8,128)}, u32[]{:S(2)}) copy-start(f32[8,3,128,256]{3,2,1,0:T(8,128)} %copy-done.31) | copy-start | bytes 9437188
  120.6 3.4 %copy-start.38 = (bf16[3,1024,384]{2,1,0:T(8,128)(2,1)S(1)}, bf16[3,1024,384]{2,1,0:T(8,128)(2,1)}, u32[]{:S(2)}) copy-start(bf16[3,1024,384]{2,1,0:T(8,128)(2,1)} %copy-done.37) | copy-start | bytes 7077892
  123.9 8.7 %collective-permute-start.5 = (bf16[4,4,4,48,384]{4,3,2,1,0:T(8,128)(2,1)S(1)}, bf16[4,4,4,48,384]{4,3,2,1,0:T(8,128)(2,1)S(1)}, u32[]{:S(2)}, u32[]{:S(2)}) collective-permute-start(bf16[4,4,4,48,384]{4,3,2,1,0:T(8,128)(2,1)S(1)} %attn_wgrad.2), channel_id=1, source_target_pairs={{0,1},{1,0},{2,3},{3,2},{4,5},{5,4},{6,7},{7,6},{8,9},{9,8},{10,11... | collective-permute-start | bytes 7077896 | tf_op jit(solution)/shard_map/ppermute | solution.py:510
  124.1 8.6 %copy-start.30 = (bf16[1024,384]{1,0:T(8,128)(2,1)S(1)}, bf16[1024,384]{1,0:T(8,128)(2,1)}, u32[]{:S(2)}) copy-start(bf16[1024,384]{1,0:T(8,128)(2,1)} %copy-done.29) | copy-start | bytes 2359300
  136.0 1.4 copy-start.12
  137.4 1.4 copy-start.15
  138.8 1.4 copy-start.1
  138.8 80.7 %reduce-scatter.23.cloned.1.call-start = ((), (), s32[]{:S(2)}) async-start(), calls=%async_computation.11 | async-start | bytes 2949120
  140.2 1.9 copy-start.28
  142.1 8.5 %copy-start.35 = (bf16[1024,1536]{1,0:T(8,128)(2,1)S(1)}, bf16[1024,1536]{1,0:T(8,128)(2,1)}, u32[]{:S(2)}) copy-start(bf16[1024,1536]{1,0:T(8,128)(2,1)} %get-tuple-element.64.lhs_ref) | copy-start | bytes 9437188
  146.0 4.7 %collective-permute-start.7 = (bf16[4,4,96,768]{3,2,1,0:T(8,128)(2,1)S(1)}, bf16[4,4,96,768]{3,2,1,0:T(8,128)(2,1)S(1)}, u32[]{:S(2)}, u32[]{:S(2)}) collective-permute-start(bf16[4,4,96,768]{3,2,1,0:T(8,128)(2,1)S(1)} %wgrad.6), channel_id=1, source_target_pairs={{0,1},{1,0},{2,3},{3,2},{4,5},{5,4},{6,7},{7,6},{8,9},{9,8},{10,11... | collective-permute-start | bytes 7077896 | tf_op jit(solution)/shard_map/ppermute | solution.py:510
  154.7 1.4 copy-start.16
  156.1 1.5 copy-start.21
  156.1 103.9 %reduce-scatter.21.cloned.1.call-start = ((), (), s32[]{:S(2)}) async-start(), calls=%async_computation.10 | async-start | bytes 2949120
  157.6 2.0 copy-start.5
  159.5 7.8 %copy-start.7 = (bf16[1024,1536]{1,0:T(8,128)(2,1)S(1)}, bf16[1024,1536]{1,0:T(8,128)(2,1)}, u32[]{:S(2)}) copy-start(bf16[1024,1536]{1,0:T(8,128)(2,1)} %copy-done.6) | copy-start | bytes 9437188
  162.7 4.6 %collective-permute-start.6 = (bf16[4,4,48,1536]{3,2,1,0:T(8,128)(2,1)S(1)}, bf16[4,4,48,1536]{3,2,1,0:T(8,128)(2,1)S(1)}, u32[]{:S(2)}, u32[]{:S(2)}) collective-permute-start(bf16[4,4,48,1536]{3,2,1,0:T(8,128)(2,1)S(1)} %wgrad.4), channel_id=1, source_target_pairs={{0,1},{1,0},{2,3},{3,2},{4,5},{5,4},{6,7},{7,6},{8,9},{9,8},{10,11... | collective-permute-start | bytes 7077896 | tf_op jit(solution)/shard_map/ppermute | solution.py:510
  170.6 1.4 copy-start.14
  172.1 47.5 %copy-start.45 = (f32[3,8,768]{2,1,0:T(8,128)S(1)}, f32[3,8,768]{2,1,0:T(8,128)}, u32[]{:S(2)}) copy-start(f32[3,8,768]{2,1,0:T(8,128)} %get-tuple-element.67) | copy-start | bytes 221188
  172.1 63.0 %copy-start.11 = (bf16[3,1024,384]{2,1,0:T(8,128)(2,1)S(1)}, bf16[3,1024,384]{2,1,0:T(8,128)(2,1)}, u32[]{:S(2)}) copy-start(bf16[3,1024,384]{2,1,0:T(8,128)(2,1)} %copy-done.10) | copy-start | bytes 7077892
  172.1 112.1 %reduce-scatter.13.cloned.1.call-start = ((), (), s32[]{:S(2)}) async-start(), calls=%async_computation.6 | async-start | bytes 737280 | tf_op jit(solution)/shard_map/reduce_scatter | solution.py:554
  179.1 127.7 %reduce-scatter.17.cloned.1.call-start = ((), (), s32[]{:S(2)}) async-start(), calls=%async_computation.8 | async-start | bytes 737280 | tf_op jit(solution)/shard_map/reduce_scatter | solution.py:554
  219.6 109.7 %reduce-scatter.15.cloned.1.call-start = ((), (), s32[]{:S(2)}) async-start(), calls=%async_computation.7 | async-start | bytes 737280 | tf_op jit(solution)/shard_map/reduce_scatter | solution.py:554
  219.8 1.3 collective-permute-start.8
  221.1 3.9 %collective-permute-start.9 = (f32[6912]{0:T(1024)S(1)}, f32[6912]{0:T(1024)S(1)}, u32[]{:S(2)}, u32[]{:S(2)}) collective-permute-start(f32[6912]{0:T(1024)S(1)} %fusion.1), channel_id=1, source_target_pairs={{0,2},{2,0},{4,6},{6,4},{8,10},{10,8},{12,14},{14,12},{16,18},{18,... | collective-permute-start | bytes 82952 | tf_op jit(solution)/shard_map/ppermute | solution.py:570
  224.9 3.9 %collective-permute-start.10 = (f32[6912]{0:T(1024)S(1)}, f32[6912]{0:T(1024)S(1)}, u32[]{:S(2)}, u32[]{:S(2)}) collective-permute-start(f32[6912]{0:T(1024)S(1)} %add.39), channel_id=1, source_target_pairs={{0,4},{2,6},{4,0},{6,2},{8,12},{10,14},{12,8},{14,10},{16,20},{18,... | collective-permute-start | bytes 82952 | tf_op jit(solution)/shard_map/ppermute | solution.py:570
  228.8 3.9 %collective-permute-start.11 = (f32[6912]{0:T(1024)S(1)}, f32[6912]{0:T(1024)S(1)}, u32[]{:S(2)}, u32[]{:S(2)}) collective-permute-start(f32[6912]{0:T(1024)S(1)} %add.40), channel_id=1, source_target_pairs={{0,8},{2,10},{4,12},{6,14},{8,0},{10,2},{12,4},{14,6},{16,24},{18,... | collective-permute-start | bytes 82952 | tf_op jit(solution)/shard_map/ppermute | solution.py:570
  232.7 16.3 %collective-permute-start.12 = (f32[6912]{0:T(1024)S(1)}, f32[6912]{0:T(1024)S(1)}, u32[]{:S(2)}, u32[]{:S(2)}) collective-permute-start(f32[6912]{0:T(1024)S(1)} %add.41), channel_id=1, source_target_pairs={{0,16},{2,18},{4,20},{6,22},{8,24},{10,26},{12,28},{14,30},{16,0},... | collective-permute-start | bytes 82952 | tf_op jit(solution)/shard_map/ppermute | solution.py:570
  235.1 1.8 copy-start.13
  236.9 1.6 copy-start.18
  238.5 1.6 copy-start.20
  240.1 1.9 copy-start.27
  (1 other events, 0.9 us)
Sparse Core Ops, SparseCore 0:
  139.0 40.0 reduce-scatter.18
  182.1 37.3 reduce-scatter.22
  222.6 37.3 reduce-scatter.20
  262.2 22.0 reduce-scatter.12
  286.3 20.3 reduce-scatter.16
  308.9 20.3 reduce-scatter.14
